TPU v7x, 32 devices: a whole 2x2x4 slice. The times are simulated.
32 devices in a mesh: groups: 2 (over x), sector: 16 (over z, y, core).
Axes of the slice: x: 2, y: 2, z: 4, core: 2. Of those that a mesh axis runs over, the one named last changes fastest.
Arguments:
- wavefunction: bfloat16 [8192, 1024], P(('groups', 'sector')), parts along dimension 0, may hold values from -6 to 6
- widths: int32 [32], P(('groups', 'sector')), parts along dimension 0, may hold values from 1 to 256, 2048 in all
- env_left: bfloat16 [26, 256, 8192], P(None, None, ('groups', 'sector')), parts along dimension 2, may hold values from -0.078125 to 0.078125
- env_right: bfloat16 [52, 64, 64], P('groups'), parts along dimension 0, may hold values from -0.75 to 0.75
- site_tensor: bfloat16 [26, 26, 16, 16], replicated, may hold values from -0.3125 to 0.3125
- shift_class: int32 [26], replicated, may hold values from 0 to 4, as said below
Outputs:
- sigma: bfloat16 [8192, 1024], P(('groups', 'sector')), parts along dimension 0
There are 2 independent parts, one for each index of `groups`. A program takes and returns all parts, laid end to end along the dimension named above; an argument that names none is the same for every part. Nothing has to cross between parts.
Inputs may be any that keep to these rules, and one draw needn't show every extreme that they name: The widths of the 16 sectors sum to 2048, and one of them equals 256. `shift_class`: each class 0 to 4 is held by at least 5 channels.
All inputs are finite; a program needn't handle non-finite values. No bound on the sum of `widths` on one device may be relied on, other than what follows from the above.
Results may differ from a plain program's by a relative error of at most 0.0058.
Values sent between devices are 32-bit elements; how exact they have to be, the bound alone decides.
A program may use at most 192 MiB of HBM per device.

v0:
```python
import functools

import jax
import jax.numpy as jnp
from jax import lax
from jax.experimental import pallas as pl
from jax.experimental.pallas import tpu as pltpu
from jax.sharding import PartitionSpec as P

DOWNS = 8
CLASSES = 5
CHUNKS = 4
VPAD = 32
MESH = pl.DeviceIdType.MESH
F32 = jnp.float32
BF16 = jnp.bfloat16


def kernel(
    count,
    order_ref,
    width_ref,
    wave_ref,
    envr_ref,
    site_ref,
    env_hbm,
    out_ref,
    env_ref,
    wave_t,
    right_f32,
    right_t,
    mixer,
    right_done,
    site_done,
    terms,
    landed,
    total,
    env_sem,
    send_sem,
    recv_sem,
):
    rows, cols = wave_ref.shape
    channels, _, states, _ = site_ref.shape
    window = envr_ref.shape[1]
    qs = window // CHUNKS
    block = qs * states
    slots = order_ref.shape[0] // (2 * CLASSES)
    me = lax.axis_index("sector")
    down = lax.rem(me, DOWNS)
    offsets = (DOWNS, -DOWNS, 1, -1)
    sends = (me + DOWNS < count, me >= DOWNS, down != DOWNS - 1, down != 0)
    takes = (me >= DOWNS, me + DOWNS < count, down != 0, down != DOWNS - 1)

    env_copy = pltpu.make_async_copy(env_hbm, env_ref, env_sem)
    env_copy.start()
    barrier = pltpu.get_barrier_semaphore()
    for i in range(4):

        @pl.when(sends[i])
        def _():
            pl.semaphore_signal(
                barrier, inc=1, device_id={"sector": me + offsets[i]}, device_id_type=MESH
            )

    live = lax.broadcasted_iota(jnp.int32, (128, rows), 1) < width_ref[0]
    for i in range(cols // 128):
        part = wave_ref[:, i * 128 : (i + 1) * 128].astype(F32).T
        wave_t[i * 128 : (i + 1) * 128, :] = jnp.where(live, part, 0.0).astype(BF16)

    right_f32[...] = jnp.zeros_like(right_f32)
    for v in range(channels):
        flipped = envr_ref[v].astype(F32).T
        wide = jnp.concatenate([flipped, jnp.zeros((window, 128 - window), F32)], axis=1)
        right_f32[pl.ds(v, window, stride=VPAD), :] = wide
    right_t[...] = right_f32[...].astype(BF16)

    depth = states * VPAD
    spot_s = lax.broadcasted_iota(jnp.int32, (states, depth), 0)
    spot_c = lax.broadcasted_iota(jnp.int32, (states, depth), 1)
    packed = jnp.zeros((channels * states, depth), F32)
    for v in range(channels):
        place = (spot_c == spot_s * VPAD + v).astype(F32).astype(BF16)
        packed += jnp.dot(
            site_ref[:, v].reshape(channels * states, states), place, preferred_element_type=F32
        )
    mixer[...] = packed.astype(BF16)

    pl.semaphore_wait(barrier, sum(jnp.where(take, 1, 0) for take in takes))

    def remote(i, c):
        return pltpu.make_async_remote_copy(
            src_ref=terms.at[i, c],
            dst_ref=landed.at[i, c],
            send_sem=send_sem.at[i, c],
            recv_sem=recv_sem.at[i, c],
            device_id={"sector": me + offsets[i]},
            device_id_type=MESH,
        )

    def class_sum(k):
        acc = jnp.zeros((block, rows), F32)
        for j in range(slots):
            at = order_ref[k * slots + j]
            left = env_ref[at]
            if j >= channels // CLASSES:
                held = order_ref[(CLASSES + k) * slots + j].astype(F32)
                left = (left.astype(F32) * held).astype(BF16)
            acc += lax.dot_general(
                site_done[at], left, (((1,), (1,)), ((), ())), preferred_element_type=F32
            )
        return acc

    @pl.loop(0, CHUNKS)
    def _(c):
        right_rows = right_t[pl.ds(pl.multiple_of(c * qs * VPAD, 16), qs * VPAD), :window]
        for s in range(states):
            done = jnp.dot(
                right_rows,
                wave_t[s * window : (s + 1) * window, :],
                preferred_element_type=F32,
            ).astype(BF16)
            right_done[:, s * VPAD : (s + 1) * VPAD, :] = done.reshape(qs, VPAD, rows)
        for q in range(qs):
            done = jnp.dot(mixer[...], right_done[q], preferred_element_type=F32).astype(BF16)
            site_done[:, q * states : (q + 1) * states, :] = done.reshape(channels, states, rows)

        @pl.when(c == 0)
        def _():
            env_copy.wait()

        for i in range(4):

            @pl.when(sends[i])
            def _():
                terms[i, c] = class_sum(i + 1)
                remote(i, c).start()

        own = class_sum(0)
        at = pl.ds(pl.multiple_of(c * block, block), block)
        for h in range(rows // 128):
            total[h, at, :] = own[:, h * 128 : (h + 1) * 128]

    @pl.loop(0, CHUNKS)
    def _(c):
        at = pl.ds(pl.multiple_of(c * block, block), block)
        for i in (2, 3, 0, 1):

            @pl.when(takes[i])
            def _():
                remote(i, c).wait_recv()
                for h in range(rows // 128):
                    total[h, at, :] += landed[i, c, :, h * 128 : (h + 1) * 128]

    per = 128 // window
    for h in range(rows // 128):
        shown = lax.broadcasted_iota(jnp.int32, (128, 128), 0) + h * 128 < width_ref[0]
        for g in range(states // per):
            part = jnp.concatenate(
                [total[h, pl.ds(g * per + e, window, stride=states), :] for e in range(per)], axis=0
            )
            out_ref[h * 128 : (h + 1) * 128, g * 128 : (g + 1) * 128] = jnp.where(
                shown, part.T, 0.0
            ).astype(BF16)

    @pl.loop(0, CHUNKS)
    def _(c):
        for i in range(4):

            @pl.when(sends[i])
            def _():
                remote(i, c).wait_send()


def local(count, wavefunction, widths, env_left, env_right, site_tensor, shift_class):
    rows, cols = wavefunction.shape
    channels = site_tensor.shape[0]
    states = site_tensor.shape[2]
    window = env_right.shape[1]
    slots = channels - (CLASSES - 1) * (channels // CLASSES)
    ids = jnp.arange(channels, dtype=jnp.int32)
    same = shift_class[:, None] == shift_class[None, :]
    ranking = jnp.sum((same & (ids[None, :] < ids[:, None])).astype(jnp.int32), axis=1)
    slot_ids = jnp.arange(CLASSES * slots, dtype=jnp.int32)
    member = (shift_class[None, :] * slots + ranking[None, :] == slot_ids[:, None]).astype(jnp.int32)
    order = jnp.sum(jnp.stack([member * ids[None, :], member]), axis=2).reshape(-1)
    qs = window // CHUNKS
    block = qs * states
    vmem = pl.BlockSpec(memory_space=pltpu.VMEM)
    smem = pl.BlockSpec(memory_space=pltpu.SMEM)
    return pl.pallas_call(
        functools.partial(kernel, count),
        out_shape=jax.ShapeDtypeStruct((rows, cols), BF16),
        in_specs=[smem, smem, vmem, vmem, vmem, pl.BlockSpec(memory_space=pl.ANY)],
        out_specs=vmem,
        scratch_shapes=[
            pltpu.VMEM((channels, rows, rows), BF16),
            pltpu.VMEM((cols, rows), BF16),
            pltpu.VMEM((window * VPAD, 128), F32),
            pltpu.VMEM((window * VPAD, 128), BF16),
            pltpu.VMEM((channels * states, states * VPAD), BF16),
            pltpu.VMEM((qs, states * VPAD, rows), BF16),
            pltpu.VMEM((channels, block, rows), BF16),
            pltpu.VMEM((4, CHUNKS, block, rows), F32),
            pltpu.VMEM((4, CHUNKS, block, rows), F32),
            pltpu.VMEM((rows // 128, cols, 128), F32),
            pltpu.SemaphoreType.DMA,
            pltpu.SemaphoreType.DMA((4, CHUNKS)),
            pltpu.SemaphoreType.DMA((4, CHUNKS)),
        ],
        compiler_params=pltpu.CompilerParams(
            collective_id=0, has_side_effects=True, vmem_limit_bytes=56 * 1024 * 1024
        ),
        cost_estimate=pl.CostEstimate(
            flops=10_000_000_000, bytes_accessed=8_000_000, transcendentals=0
        ),
    )(order, widths, wavefunction, env_right, site_tensor, env_left)


def solution(mesh):
    placed = (
        P(("groups", "sector"), None),
        P(("groups", "sector")),
        P(None, None, ("groups", "sector")),
        P("groups", None, None),
        P(),
        P(),
    )
    return jax.shard_map(
        functools.partial(local, mesh.shape["sector"]),
        mesh=mesh,
        in_specs=placed,
        out_specs=P(("groups", "sector"), None),
        check_vma=False,
    )
```

profile of v0, /device:TPU:0, one launch (start us, length us, event | category | flops | bytes accessed | tf_op | source)
XLA Modules:
  0.0 70.4 jit_solution(11535865527888777597)
XLA Ops:
  0.7 0.9 %convert_reduce_fusion = s32[26]{0:T(128)S(1)} fusion(s32[26]{0:T(128)} %param.11), kind=kLoop, calls=%fused_computation.3 | loop fusion | flops 3354 | bytes 208 | tf_op jit(solution)/shard_map/reduce_sum | solution.py:182
  1.6 0.7 multiply_add_fusion
  2.2 0.1 compare_convert_fusion
  2.3 0.1 compare_select_fusion
  2.5 0.6 reshape.74.order_ref
  3.1 5.3 %copy.8.site_ref = bf16[26,26,16,16]{3,2,1,0:T(8,128)(2,1)} copy(bf16[26,26,16,16]{1,3,2,0:T(8,128)(2,1)} %param.10) | data formatting | bytes 692224 | tf_op args[4]
  8.4 60.2 %shard_map.64 = bf16[256,1024]{1,0:T(8,128)(2,1)} custom-call(s32[60]{0:T(128)} %reshape.74.order_ref, s32[1]{0:T(128)S(6)} %copy.10.width_ref, bf16[256,1024]{1,0:T(8,128)(2,1)} %wave_ref.1, bf16[26,64,64]{2,1,0:T(8,128)(2,1)} %envr_ref.1, bf16[26,26,16,16]{3,2,1,0:T(8,128)(2,1)} %copy.8.site_ref, bf16[26,256,256]{2,1,0:T(8,128)(2,1)} %env_hbm.1), custom_call_target="tpu_custom_call" | custom-call | flops 10000000000 | bytes 8000000 | tf_op jit(solution)/shard_map/pallas_call | solution.py:190
  68.6 1.9 %copy.11 = bf16[256,1024]{1,0:T(8,128)(2,1)} copy(bf16[256,1024]{1,0:T(8,128)(2,1)} %shard_map.64) | data formatting | bytes 1048576
  (1 shorter events, 0.0 us)
where the time goes:
time: 70.7 us; the launch traced here: 70.4 us
  Pallas kernels  60.2 us (85%)
  local copies, waits for them, and re-layouts  7.76 us (11%)
  other arithmetic  1.8 us (3%)
    pallas_call x1, Pallas kernels, local(): pl.pallas_call(functools.partial(kernel, count), out_shape=jax.ShapeDtype...  60.2 us
    unnamed x2, local copies, waits for them, and re-layouts  7.17 us

commit v1 on v0

v1 whole, which is shorter than its diff:
```python
import functools

import jax
import jax.numpy as jnp
from jax import lax
from jax.experimental import pallas as pl
from jax.experimental.pallas import tpu as pltpu
from jax.sharding import PartitionSpec as P

DOWNS = 8
CLASSES = 5
CHUNKS = 8
VPAD = 32
MESH = pl.DeviceIdType.MESH
F32 = jnp.float32
BF16 = jnp.bfloat16


def kernel(
    count,
    class_ref,
    wave_hbm,
    envr_hbm,
    site_hbm,
    env_hbm,
    width_ref,
    out_ref,
    wave_ref,
    envr_ref,
    site_ref,
    env_ref,
    wave_t,
    right_f32,
    stage,
    mixer,
    right_done,
    site_done,
    terms,
    landed,
    total,
    load_sem,
    send_sem,
    recv_sem,
):
    rows, cols = wave_ref.shape
    channels, states, _, _ = site_ref.shape
    window = envr_ref.shape[1]
    qs = window // CHUNKS
    block = qs * states
    slots = stage.shape[0] // (states * states)
    mixed = slots * states
    me = lax.axis_index("sector")
    down = lax.rem(me, DOWNS)
    offsets = (DOWNS, -DOWNS, 1, -1)
    sends = (me + DOWNS < count, me >= DOWNS, down != DOWNS - 1, down != 0)
    takes = (me >= DOWNS, me + DOWNS < count, down != 0, down != DOWNS - 1)

    loads = [
        pltpu.make_async_copy(source, target, load_sem.at[i])
        for i, (source, target) in enumerate(
            ((wave_hbm, wave_ref), (envr_hbm, envr_ref), (site_hbm, site_ref), (env_hbm, env_ref))
        )
    ]
    for load in loads:
        load.start()
    barrier = pltpu.get_barrier_semaphore()
    for i in range(4):

        @pl.when(sends[i])
        def _():
            pl.semaphore_signal(
                barrier, inc=1, device_id={"sector": me + offsets[i]}, device_id_type=MESH
            )

    def members(k):
        found = [jnp.int32(0)] * slots
        upto = jnp.int32(0)
        for w in range(channels):
            upto = upto + jnp.where(class_ref[w] == k, 1, 0)
            found = [spot + jnp.where(upto <= j, 1, 0) for j, spot in enumerate(found)]
        return found

    order = [members(k) for k in (1, 2, 3, 4, 0)]

    def build_mixer(p):
        for j in range(slots):
            at = jnp.minimum(order[p][j], channels - 1)
            held = jnp.where(order[p][j] < channels, 1.0, 0.0)
            piece = site_ref[at].reshape(states * states, channels).astype(F32) * held
            wide = jnp.concatenate(
                [piece, jnp.zeros((states * states, 128 - channels), F32)], axis=1
            )
            stage[j * states * states : (j + 1) * states * states, :] = wide
        per = 128 // VPAD
        for g in range(states // per):
            part = jnp.concatenate(
                [
                    stage[pl.ds(g * per + e, mixed, stride=states), :][:, :VPAD]
                    for e in range(per)
                ],
                axis=1,
            )
            mixer[p * mixed : (p + 1) * mixed, g * 128 : (g + 1) * 128] = part.astype(BF16)

    def apply_right(c):
        right_rows = right_f32[
            pl.ds(pl.multiple_of(c * qs * VPAD, 16), qs * VPAD), :window
        ].astype(BF16)
        for s in range(states):
            done = jnp.dot(
                right_rows,
                wave_t[s * window : (s + 1) * window, :],
                preferred_element_type=F32,
            ).astype(BF16)
            right_done[:, s * VPAD : (s + 1) * VPAD, :] = done.reshape(qs, VPAD, rows)

    def apply_site(first, last):
        for q in range(qs):
            done = jnp.dot(
                mixer[first * mixed : last * mixed, :], right_done[q], preferred_element_type=F32
            ).astype(BF16)
            site_done[first * slots : last * slots, q * states : (q + 1) * states, :] = (
                done.reshape((last - first) * slots, states, rows)
            )

    def class_sum(p):
        acc = jnp.zeros((block, rows), F32)
        for j in range(slots):
            acc += lax.dot_general(
                site_done[p * slots + j],
                env_ref[jnp.minimum(order[p][j], channels - 1)],
                (((1,), (1,)), ((), ())),
                preferred_element_type=F32,
            )
        return acc

    def remote(i, c):
        return pltpu.make_async_remote_copy(
            src_ref=terms.at[i, c],
            dst_ref=landed.at[i, c],
            send_sem=send_sem.at[i, c],
            recv_sem=recv_sem.at[i, c],
            device_id={"sector": me + offsets[i]},
            device_id_type=MESH,
        )

    def send(i, c):
        terms[i, c] = class_sum(i)
        remote(i, c).start()

    def keep(c):
        own = class_sum(CLASSES - 1)
        at = pl.ds(pl.multiple_of(c * block, block), block)
        for h in range(rows // 128):
            total[h, at, :] = own[:, h * 128 : (h + 1) * 128]

    loads[0].wait()
    live = lax.broadcasted_iota(jnp.int32, (128, rows), 1) < width_ref[0]
    for i in range(cols // 128):
        part = wave_ref[:, i * 128 : (i + 1) * 128].astype(F32).T
        wave_t[i * 128 : (i + 1) * 128, :] = jnp.where(live, part, 0.0).astype(BF16)

    right_f32[...] = jnp.zeros_like(right_f32)
    loads[1].wait()
    for v in range(channels):
        flipped = envr_ref[v].astype(F32).T
        wide = jnp.concatenate([flipped, jnp.zeros((window, 128 - window), F32)], axis=1)
        right_f32[pl.ds(v, window, stride=VPAD), :] = wide
    apply_right(0)

    loads[2].wait()
    loads[3].wait()
    pl.semaphore_wait(barrier, sum(jnp.where(take, 1, 0) for take in takes))
    for i in range(2):

        @pl.when(sends[i])
        def _():
            build_mixer(i)
            apply_site(i, i + 1)
            send(i, 0)

        @pl.when(jnp.logical_not(sends[i]))
        def _():
            mixer[i * mixed : (i + 1) * mixed, :] = jnp.zeros((mixed, mixer.shape[1]), BF16)

    for p in range(2, CLASSES):
        build_mixer(p)
    apply_site(2, CLASSES)
    for i in range(2, 4):

        @pl.when(sends[i])
        def _():
            send(i, 0)

    keep(0)

    @pl.loop(1, CHUNKS)
    def _(c):
        apply_right(c)
        apply_site(0, CLASSES)
        for i in range(4):

            @pl.when(sends[i])
            def _():
                send(i, c)

        keep(c)

    @pl.loop(0, CHUNKS)
    def _(c):
        at = pl.ds(pl.multiple_of(c * block, block), block)
        for i in (2, 3, 0, 1):

            @pl.when(takes[i])
            def _():
                remote(i, c).wait_recv()
                for h in range(rows // 128):
                    total[h, at, :] += landed[i, c, :, h * 128 : (h + 1) * 128]

    per = 128 // window
    for h in range(rows // 128):
        shown = lax.broadcasted_iota(jnp.int32, (128, 128), 0) + h * 128 < width_ref[0]
        for g in range(states // per):
            part = jnp.concatenate(
                [total[h, pl.ds(g * per + e, window, stride=states), :] for e in range(per)], axis=0
            )
            out_ref[h * 128 : (h + 1) * 128, g * 128 : (g + 1) * 128] = jnp.where(
                shown, part.T, 0.0
            ).astype(BF16)

    @pl.loop(0, CHUNKS)
    def _(c):
        for i in range(4):

            @pl.when(sends[i])
            def _():
                remote(i, c).wait_send()


def local(count, wavefunction, widths, env_left, env_right, site_tensor, shift_class):
    rows, cols = wavefunction.shape
    channels = site_tensor.shape[0]
    states = site_tensor.shape[2]
    window = env_right.shape[1]
    slots = channels - (CLASSES - 1) * (channels // CLASSES)
    qs = window // CHUNKS
    block = qs * states
    vmem = pl.BlockSpec(memory_space=pltpu.VMEM)
    smem = pl.BlockSpec(memory_space=pltpu.SMEM)
    anywhere = pl.BlockSpec(memory_space=pl.ANY)
    return pl.pallas_call(
        functools.partial(kernel, count),
        out_shape=jax.ShapeDtypeStruct((rows, cols), BF16),
        in_specs=[smem, anywhere, anywhere, anywhere, anywhere, smem],
        out_specs=vmem,
        scratch_shapes=[
            pltpu.VMEM((rows, cols), BF16),
            pltpu.VMEM((channels, window, window), BF16),
            pltpu.VMEM((channels, states, states, channels), BF16),
            pltpu.VMEM((channels, rows, rows), BF16),
            pltpu.VMEM((cols, rows), BF16),
            pltpu.VMEM((window * VPAD, 128), F32),
            pltpu.VMEM((slots * states * states, 128), F32),
            pltpu.VMEM((CLASSES * slots * states, states * VPAD), BF16),
            pltpu.VMEM((qs, states * VPAD, rows), BF16),
            pltpu.VMEM((CLASSES * slots, block, rows), BF16),
            pltpu.VMEM((4, CHUNKS, block, rows), F32),
            pltpu.VMEM((4, CHUNKS, block, rows), F32),
            pltpu.VMEM((rows // 128, cols, 128), F32),
            pltpu.SemaphoreType.DMA((4,)),
            pltpu.SemaphoreType.DMA((4, CHUNKS)),
            pltpu.SemaphoreType.DMA((4, CHUNKS)),
        ],
        compiler_params=pltpu.CompilerParams(
            collective_id=0, has_side_effects=True, vmem_limit_bytes=56 * 1024 * 1024
        ),
        cost_estimate=pl.CostEstimate(
            flops=10_000_000_000, bytes_accessed=8_000_000, transcendentals=0
        ),
    )(
        shift_class,
        wavefunction,
        env_right,
        site_tensor.transpose(0, 2, 3, 1),
        env_left,
        widths,
    )


def solution(mesh):
    placed = (
        P(("groups", "sector"), None),
        P(("groups", "sector")),
        P(None, None, ("groups", "sector")),
        P("groups", None, None),
        P(),
        P(),
    )
    return jax.shard_map(
        functools.partial(local, mesh.shape["sector"]),
        mesh=mesh,
        in_specs=placed,
        out_specs=P(("groups", "sector"), None),
        check_vma=False,
    )
```

time: 70.7 us -> 58.8 us (0.83)
  local copies, waits for them, and re-layouts: 7.76 us -> 1.87 us
  Pallas kernels: 60.2 us -> 56.1 us
  other arithmetic: 1.8 us -> 0 us
    unnamed x2 -> x1, local copies, waits for them, and re-layouts: 7.17 us -> 1.87 us
    pallas_call x1, Pallas kernels: 60.2 us -> 56.1 us  [local(): pl.pallas_call(functools.partial(kernel, count), out_shape=jax.ShapeDtype...]
    reduce_sum x2 -> x0, other arithmetic: 0.95 us -> none  [the longest x1 0.91 us: local(): jnp.sum((same & (ids[None, :] < ids[:, None])).astype(jnp.int32), axis=1)]
where the time goes in v1:
time: 58.8 us; the launch traced here: 58.6 us
  Pallas kernels  56.1 us (95%)
  local copies, waits for them, and re-layouts  1.87 us (3%)
  between operations  0.66 us (1%)
    pallas_call x1, Pallas kernels, local(): pl.pallas_call(functools.partial(kernel, count), out_shape=jax.ShapeDtype...  56.1 us
    unnamed x1, local copies, waits for them, and re-layouts  1.87 us

profile of v1, /device:TPU:0, one launch (start us, length us, event | category | flops | bytes accessed | tf_op | source)
XLA Modules:
  0.0 58.6 jit_solution(2075118627412846190)
XLA Ops:
  0.7 56.1 %shard_map.64 = bf16[256,1024]{1,0:T(8,128)(2,1)} custom-call(s32[26]{0:T(128)} %class_ref.1, bf16[256,1024]{1,0:T(8,128)(2,1)} %wave_hbm.1, bf16[26,64,64]{2,1,0:T(8,128)(2,1)} %envr_hbm.1, bf16[26,16,16,26]{3,2,1,0:T(8,128)(2,1)} %bitcast.1, bf16[26,256,256]{2,1,0:T(8,128)(2,1)} %env_hbm.1, s32[1]{0:T(128)S(6)} %copy.8.width_ref), custom_call_target="tpu_custom_call" | custom-call | flops 10000000000 | bytes 8000000 | tf_op jit(solution)/shard_map/pallas_call | solution.py:251
  56.7 1.9 %copy.9 = bf16[256,1024]{1,0:T(8,128)(2,1)} copy(bf16[256,1024]{1,0:T(8,128)(2,1)} %shard_map.64) | data formatting | bytes 1048576

commit v2 on v1

--- a/solution.py
+++ b/solution.py
@@ -11,6 +11,7 @@
 CLASSES = 5
 CHUNKS = 8
 VPAD = 32
+LOADS = 6
 MESH = pl.DeviceIdType.MESH
 F32 = jnp.float32
 BF16 = jnp.bfloat16
@@ -55,11 +56,16 @@
     sends = (me + DOWNS < count, me >= DOWNS, down != DOWNS - 1, down != 0)
     takes = (me >= DOWNS, me + DOWNS < count, down != 0, down != DOWNS - 1)
 
+    half = channels // 2
+    edges = [channels * i // LOADS for i in range(LOADS + 1)]
+    pairs = [(wave_hbm, wave_ref), (envr_hbm, envr_ref)]
+    for lo, hi in ((0, half), (half, channels)):
+        pairs.append((site_hbm.at[lo:hi], site_ref.at[lo:hi]))
+    for lo, hi in zip(edges[:-1], edges[1:]):
+        pairs.append((env_hbm.at[lo:hi], env_ref.at[lo:hi]))
     loads = [
         pltpu.make_async_copy(source, target, load_sem.at[i])
-        for i, (source, target) in enumerate(
-            ((wave_hbm, wave_ref), (envr_hbm, envr_ref), (site_hbm, site_ref), (env_hbm, env_ref))
-        )
+        for i, (source, target) in enumerate(pairs)
     ]
     for load in loads:
         load.start()
@@ -168,8 +174,8 @@
         right_f32[pl.ds(v, window, stride=VPAD), :] = wide
     apply_right(0)
 
-    loads[2].wait()
-    loads[3].wait()
+    for load in loads[2:]:
+        load.wait()
     pl.semaphore_wait(barrier, sum(jnp.where(take, 1, 0) for take in takes))
     for i in range(2):
 
@@ -267,7 +273,7 @@
             pltpu.VMEM((4, CHUNKS, block, rows), F32),
             pltpu.VMEM((4, CHUNKS, block, rows), F32),
             pltpu.VMEM((rows // 128, cols, 128), F32),
-            pltpu.SemaphoreType.DMA((4,)),
+            pltpu.SemaphoreType.DMA((4 + LOADS,)),
             pltpu.SemaphoreType.DMA((4, CHUNKS)),
             pltpu.SemaphoreType.DMA((4, CHUNKS)),
         ],

time: 58.8 us -> 58.7 us (level)
  no operation moved by 1% of the time
where the time goes in v2:
time: 58.7 us; the launch traced here: 58.6 us
  Pallas kernels  56 us (95%)
  local copies, waits for them, and re-layouts  1.87 us (3%)
  between operations  0.66 us (1%)
    pallas_call x1, Pallas kernels, local(): pl.pallas_call(functools.partial(kernel, count), out_shape=jax.ShapeDtype...  56 us
    unnamed x1, local copies, waits for them, and re-layouts  1.87 us

profile of v2, /device:TPU:0, one launch (start us, length us, event | category | flops | bytes accessed | tf_op | source)
XLA Modules:
  0.0 58.6 jit_solution(17507969601279871326)
XLA Ops:
  0.7 56.0 %shard_map.64 = bf16[256,1024]{1,0:T(8,128)(2,1)} custom-call(s32[26]{0:T(128)} %class_ref.1, bf16[256,1024]{1,0:T(8,128)(2,1)} %wave_hbm.1, bf16[26,64,64]{2,1,0:T(8,128)(2,1)} %envr_hbm.1, bf16[26,16,16,26]{3,2,1,0:T(8,128)(2,1)} %bitcast.1, bf16[26,256,256]{2,1,0:T(8,128)(2,1)} %env_hbm.1, s32[1]{0:T(128)S(6)} %copy.8.width_ref), custom_call_target="tpu_custom_call" | custom-call | flops 10000000000 | bytes 8000000 | tf_op jit(solution)/shard_map/pallas_call | solution.py:257
  56.7 1.9 %copy.9 = bf16[256,1024]{1,0:T(8,128)(2,1)} copy(bf16[256,1024]{1,0:T(8,128)(2,1)} %shard_map.64) | data formatting | bytes 1048576
